TPU v7x, 256 devices: a whole 4x4x8 slice. The times are simulated.
256 devices in a mesh: dp: 8 (over z_hi, y), fsdp: 32 (over z_lo, x, core).
Axes of the slice: x: 4, y: 4, z: 8 (z_hi: 2, z_lo: 4; z = z_hi * 4 + z_lo), core: 2. Of those that a mesh axis runs over, the one named last changes fastest.
Arguments:
- partial_grads: bfloat16 [8, 16, 56, 256, 256], P('dp', None, None, 'fsdp'), may hold values from -6 to 6
- owners: int32 [16, 56], replicated, may hold values from 0 to 191, as said below
- left_roots: bfloat16 [8, 192, 256, 256], P('dp', 'fsdp'), may hold values from -0.5 to 1.5, as said below
- right_roots: bfloat16 [8, 192, 256, 256], P('dp', 'fsdp'), may hold values from -0.5 to 1.5, as said below
- left_stats: float32 [8, 192, 256, 256], P('dp', 'fsdp'), may hold values from -1 to 4, as said below
- right_stats: float32 [8, 192, 256, 256], P('dp', 'fsdp'), may hold values from -1 to 4, as said below
Outputs:
- update: bfloat16 [16, 56, 256, 256], P(None, 'dp', 'fsdp')
- new_left_stats: float32 [8, 192, 256, 256], P('dp', 'fsdp')
- new_right_stats: float32 [8, 192, 256, 256], P('dp', 'fsdp')
Inputs may be any that keep to these rules, and one draw needn't show every extreme that they name: `owners`: within the blocks of one index of dp (block columns g * 7 to (g + 1) * 7 - 1) no two blocks share a value; a value v names slot v % 6 of device v // 6 along fsdp, so each device holds at most 6 blocks of its index of dp, and in every index of dp some device holds exactly 6. `left_roots`: symmetric in the last two dimensions. `right_roots`: symmetric in the last two dimensions. `left_stats`: symmetric in the last two dimensions. `right_stats`: symmetric in the last two dimensions.
All inputs are finite; a program needn't handle non-finite values.
Results may differ from a plain program's by a relative error of at most 0.02.
Values may be sent and summed in bfloat16 or wider, within the bound.
A program may use at most 64 MiB of HBM per device.

v0:
```python
import jax
import jax.numpy as jnp
from jax import lax
from jax.sharding import PartitionSpec as P

decay = 0.95


def body(partial_grads, owners, left_roots, right_roots, left_stats, right_stats):
    groups = lax.axis_size("dp")
    owner_count = lax.axis_size("fsdp")
    slot_count = left_stats.shape[1]
    block_size = left_stats.shape[2]
    strip_rows = block_size // owner_count
    row_blocks = owners.shape[0]
    per_group = owners.shape[1] // groups
    total_slots = slot_count * owner_count
    slot_order = (
        jnp.arange(slot_count, dtype=jnp.int32)[:, None]
        + slot_count * jnp.arange(owner_count, dtype=jnp.int32)[None, :]
    ).reshape(-1)
    group_index = lax.axis_index("dp")
    my_blocks = lax.dynamic_slice_in_dim(owners, group_index * per_group, per_group, 1).reshape(-1)
    select = (slot_order[:, None] == my_blocks[None, :]).astype(jnp.bfloat16)
    summed = lax.psum_scatter(
        partial_grads[0].astype(jnp.float32).astype(jnp.bfloat16),
        "dp",
        scatter_dimension=1,
        tiled=True,
    ).astype(jnp.float32)
    gradient = (summed / groups).astype(jnp.bfloat16)
    flat_grad = gradient.reshape(row_blocks * per_group, strip_rows * block_size)
    packed = jnp.dot(select, flat_grad, preferred_element_type=jnp.float32).astype(jnp.bfloat16)
    packed = packed.reshape(slot_count, owner_count, strip_rows, block_size)
    arrived = lax.all_to_all(packed, "fsdp", split_axis=1, concat_axis=1, tiled=True)
    blocks = arrived.reshape(slot_count, block_size, block_size)
    own_ids = lax.axis_index("fsdp") * slot_count + jnp.arange(slot_count, dtype=jnp.int32)
    occupied = jnp.any(own_ids[:, None] == my_blocks[None, :], axis=1)[:, None, None]
    outer_left = jnp.einsum("sij,skj->sik", blocks, blocks, preferred_element_type=jnp.float32)
    outer_right = jnp.einsum("sji,sjk->sik", blocks, blocks, preferred_element_type=jnp.float32)
    new_left = jnp.where(
        occupied, decay * left_stats[0] + (1.0 - decay) * outer_left, left_stats[0]
    )
    new_right = jnp.where(
        occupied, decay * right_stats[0] + (1.0 - decay) * outer_right, right_stats[0]
    )
    new_left, new_right = (new_left[None], new_right[None])
    left_half = jnp.einsum(
        "sij,sjk->sik", left_roots[0], blocks, preferred_element_type=jnp.float32
    ).astype(jnp.bfloat16)
    update = jnp.einsum(
        "sij,sjk->sik", left_half, right_roots[0], preferred_element_type=jnp.float32
    ).astype(jnp.bfloat16)
    update = update.reshape(slot_count, owner_count, strip_rows, block_size)
    returned = lax.all_to_all(update, "fsdp", split_axis=1, concat_axis=1, tiled=True)
    local_update = jnp.dot(
        select.T,
        returned.reshape(total_slots, strip_rows * block_size),
        preferred_element_type=jnp.float32,
    ).astype(jnp.bfloat16)
    local_update = local_update.reshape(row_blocks, per_group, strip_rows, block_size)
    return (local_update, new_left, new_right)


def solution(mesh):
    placed = (
        P("dp", None, None, "fsdp", None),
        P(),
        P("dp", "fsdp", None, None),
        P("dp", "fsdp", None, None),
        P("dp", "fsdp", None, None),
        P("dp", "fsdp", None, None),
    )
    return jax.shard_map(
        body,
        mesh=mesh,
        in_specs=placed,
        out_specs=(
            P(None, "dp", "fsdp", None),
            P("dp", "fsdp", None, None),
            P("dp", "fsdp", None, None),
        ),
        check_vma=False,
    )
```

profile of v0, /device:TPU:1, one launch (start us, length us, event | category | flops | bytes accessed | tf_op | source)
XLA Modules:
  0.0 263.7 jit_solution(12932102283628705997)
XLA Ops:
  7.2 0.7 all-reduce.3.cloned.1.call-update
  7.9 0.1 copy-done.3
  8.0 0.1 constant_dynamic-slice_fusion
  8.1 0.1 eq.29
  8.2 0.1 add.44
  8.3 0.6 dynamic-slice
  9.5 181.9 %all-reduce.3.cloned.1.call-done = bf16[16,56,8,256]{3,2,1,0:T(8,128)(2,1)} async-done(((bf16[16,56,8,256]{3,2,1,0:T(8,128)(2,1)}), bf16[16,56,8,256]{3,2,1,0:T(8,128)(2,1)}) %all-reduce.3.cloned.1.call-update) | async-done | bytes 3670032
  191.4 1.1 multiply_convert_fusion
  192.5 0.1 copy.37
  192.6 0.4 convolution_convert_fusion
  193.0 0.2 copy.38
  193.3 0.1 copy.25
  193.3 34.2 %all_to_all.10 = bf16[6,32,8,256]{3,2,0,1:T(8,128)(2,1)S(1)} all-to-all(bf16[6,32,8,256]{3,2,0,1:T(8,128)(2,1)S(1)} %copy.25), channel_id=1, replica_groups=mesh['dp'=8,'fsdp'=32] {'fsdp'}, dimensions={1} | all-to-all | bytes 1572864 | tf_op jit(solution)/shard_map/all_to_all | solution.py:35
  227.5 0.7 fusion.4
  228.2 0.9 copy.29
  229.1 4.6 %all-to-all-start.1 = ((bf16[6,32,8,256]{3,2,0,1:T(8,128)(2,1)}), bf16[6,32,8,256]{3,2,0,1:T(8,128)(2,1)S(1)}, u32[]{:S(2)}, u32[]{:S(2)}) async-start(bf16[6,32,8,256]{3,2,0,1:T(8,128)(2,1)} %copy.29), calls=%async_computation.1 | async-start | bytes 1572864 | tf_op jit(solution)/shard_map/all_to_all | solution.py:55
  233.8 0.2 compare_reduce_fusion
  234.0 3.2 %fusion.1 = f32[1,6,256,256]{3,2,1,0:T(8,128)} fusion(f32[1,6,256,256]{3,2,1,0:T(8,128)} %param.11, pred[6]{0:T(512)(128)(4,1)S(1)} %compare_reduce_fusion, bf16[6,32,8,256]{3,2,0,1:T(8,128)(2,1)S(1)} %all_to_all.10), kind=kOutput, calls=%fused_computation.5 | convolution fusion | flops 202899456 | bytes 3932166 | tf_op jit(solution)/shard_map/sji,sjk->sik/dot_general | solution.py:40
  237.2 1.7 fusion.3
  238.8 16.5 %all-to-all-done.1 = bf16[6,32,8,256]{3,2,0,1:T(8,128)(2,1)S(1)} async-done(((bf16[6,32,8,256]{3,2,0,1:T(8,128)(2,1)}), bf16[6,32,8,256]{3,2,0,1:T(8,128)(2,1)S(1)}, u32[]{:S(2)}, u32[]{:S(2)}) %all-to-all-start.1) | async-done | bytes 786464 | tf_op jit(solution)/shard_map/all_to_all | solution.py:55
  255.3 0.1 copy.30
  255.3 0.2 copy.39
  255.5 0.4 convolution_convert_fusion.1
  255.9 0.9 copy.40
  (13 shorter events, 0.1 us)
Async XLA Ops:
  7.2 220.3 %copy-start = (bf16[1,6,256,256]{3,2,1,0:T(8,128)(2,1)S(1)}, bf16[1,6,256,256]{3,2,1,0:T(8,128)(2,1)}, u32[]{:S(2)}) copy-start(bf16[1,6,256,256]{3,2,1,0:T(8,128)(2,1)} %param.9) | copy-start | bytes 2359300
  7.2 184.2 %all-reduce.3.cloned.1.call-start = ((), (), s32[]{:S(2)}) async-start(), calls=%async_computation.2 | async-start | bytes 7340032
  7.2 0.8 copy-start.3
  7.2 1.0 copy-start.4
  193.2 34.3 %copy-start.2 = (bf16[1,6,256,256]{3,2,1,0:T(8,128)(2,1)S(1)}, bf16[1,6,256,256]{3,2,1,0:T(8,128)(2,1)}, u32[]{:S(2)}) copy-start(bf16[1,6,256,256]{3,2,1,0:T(8,128)(2,1)} %param.8) | copy-start | bytes 2359300
  229.1 26.2 %all-to-all-start.1 = ((bf16[6,32,8,256]{3,2,0,1:T(8,128)(2,1)}), bf16[6,32,8,256]{3,2,0,1:T(8,128)(2,1)S(1)}, u32[]{:S(2)}, u32[]{:S(2)}) async-start(bf16[6,32,8,256]{3,2,0,1:T(8,128)(2,1)} %copy.29), calls=%async_computation.1 | async-start | bytes 1572864 | tf_op jit(solution)/shard_map/all_to_all | solution.py:55
  234.0 3.2 %copy-start.1 = (f32[1,6,256,256]{3,2,1,0:T(8,128)S(1)}, f32[1,6,256,256]{3,2,1,0:T(8,128)}, u32[]{:S(2)}) copy-start(f32[1,6,256,256]{3,2,1,0:T(8,128)} %param.10) | copy-start | bytes 4718596
Sparse Core Ops, SparseCore 0:
  10.7 180.6 all-reduce.2
where the time goes:
time: 264 us
  waiting for transfers between devices  199 us (75%)
  blocking collectives  34.2 us (13%)
  between operations  14.8 us (6%)
  matrix products  6.32 us (2%)
  starting transfers between devices  4.66 us (2%)
  local copies, waits for them, and re-layouts  3.3 us (1%)
    unnamed x2, waiting for transfers between devices  183 us
    all_to_all x1, blocking collectives, body(): lax.all_to_all(packed, 'fsdp', split_axis=1, concat_axis=1, tiled=True)  34.2 us
    all_to_all x1, waiting for transfers between devices, body(): lax.all_to_all(update, 'fsdp', split_axis=1, concat_axis=1, tiled=True)  16.5 us
  transfers between devices with their start and end apart: 2, of which 2 were waited for; matrix products, arithmetic and copies ran while one was open for 2% of the time, Pallas kernels for 0%

commit v1 on v0

v1 whole, which is shorter than its diff:
```python
import jax
import jax.numpy as jnp
from jax import lax
from jax.experimental import pallas as pl
from jax.experimental.pallas import tpu as pltpu
from jax.sharding import PartitionSpec as P

MESH = pl.DeviceIdType.MESH
DECAY = 0.95
BR, BCD, ROWS, B = 16, 7, 8, 256
NBG, SLOTS, NF, NY, NDP = 112, 6, 32, 4, 8
HALF = B // 2
HR = BR // 2


def kernel(
    pg, inv, own, coef, lroot, rroot, lstat, rstat,
    upd, nl, nr,
    far, raw, com, mix, near, mine, part, zout, zin, grad, snd, rcv, ret, back,
    lv, rv, lsv, rsv, nlv, nrv,
    far_s, far_r, raw_s, raw_r, com_s, com_r, near_s, mine_s, z_s, z_r,
    a_s, a_r, b_s, b_r, load_s, out_s,
):
    dp = lax.axis_index("dp")
    me = lax.axis_index("fsdp")
    zh, y = dp // NY, dp % NY
    up, down = (y + 1) % NY, (y + 3) % NY
    over = (y + 2) % NY
    to = (zh * NY + up, zh * NY + down)
    across = (1 - zh) * NY + y

    barrier = pltpu.get_barrier_semaphore()
    for d in to + (across,):
        pl.semaphore_signal(barrier, inc=1, device_id={"dp": d}, device_id_type=MESH)
    for k in range(1, NF):
        pl.semaphore_signal(
            barrier, inc=1, device_id={"fsdp": (me + k) % NF}, device_id_type=MESH
        )

    units = [(c, h) for c in range(2) for h in range(2)]

    def cut(k, rows, target):
        c, h = units[k]
        side = 1 - zh if h == 0 else zh
        g = side * NY + target
        return pg.at[rows, pl.ds(g * BCD, BCD), :, pl.ds(c * HALF, HALF)]

    first, second, both = pl.ds(0, HR), pl.ds(HR, HR), pl.ds(0, BR)
    near_cp, mine_cp = {}, {}
    for k in range(4):
        near_cp[k, 0] = pltpu.make_async_copy(cut(k, first, up), near.at[k, 0], near_s.at[k, 0])
        near_cp[k, 1] = pltpu.make_async_copy(cut(k, second, down), near.at[k, 1], near_s.at[k, 1])
        mine_cp[k] = pltpu.make_async_copy(cut(k, both, y), mine.at[k], mine_s.at[k])
    loads = [
        pltpu.make_async_copy(src, dst, load_s.at[i])
        for i, (src, dst) in enumerate(((lroot, lv), (rroot, rv), (lstat, lsv), (rstat, rsv)))
    ]
    for k in range(4):
        near_cp[k, 0].start()
        near_cp[k, 1].start()
        mine_cp[k].start()

    pl.semaphore_wait(barrier, 3 + NF - 1)

    def remote(src, dst, s, r, device):
        cp = pltpu.make_async_remote_copy(
            src_ref=src, dst_ref=dst, send_sem=s, recv_sem=r, device_id=device, device_id_type=MESH
        )
        cp.start()
        return cp

    far_cp, raw_cp, com_cp, z_cp = {}, {}, {}, {}

    def send_far(k):
        for d, rows in enumerate((first, second)):
            far_cp[k, d] = remote(
                cut(k, rows, over), far.at[k, d], far_s.at[k, d], far_r.at[k, d], {"dp": to[d]}
            )

    def send_raw(k):
        for d, (rows, target) in enumerate(((second, up), (first, down))):
            raw_cp[k, d] = remote(
                cut(k, rows, target), raw.at[k, d], raw_s.at[k, d], raw_r.at[k, d], {"dp": to[d]}
            )

    def send_com(k):
        for d in range(2):
            near_cp[k, d].wait()
            far_cp[k, d].wait_recv()

            def add(r, _):
                mix[k, d, r] = far[k, d, r] + near[k, d, r]
                return 0

            lax.fori_loop(0, HR, add, 0)
            com_cp[k, d] = remote(
                mix.at[k, d], com.at[k, d], com_s.at[k, d], com_r.at[k, d], {"dp": to[d]}
            )

    def finish(k):
        c, h = units[k]
        mine_cp[k].wait()
        for d in range(2):
            raw_cp[k, d].wait_recv()
            com_cp[k, d].wait_recv()
        f32 = jnp.float32

        def add(r, _):
            for d in range(2):
                total = mine[k, d * HR + r].astype(f32) + com[k, d, r].astype(f32)
                total = total + raw[k, 1 - d, r].astype(f32)
                if h == 0:
                    zout[c, d * HR + r] = total.astype(jnp.bfloat16)
                else:
                    part[c, d * HR + r] = total
            return 0

        lax.fori_loop(0, HR, add, 0)
        if h == 0:
            z_cp[c] = remote(zout.at[c], zin.at[c], z_s.at[c], z_r.at[c], {"dp": across})

    a_cp = {}

    def exchange(c):
        z_cp[c].wait_recv()

        def add(r, _):
            total = (part[c, r] + zin[c, r].astype(jnp.float32)) / NDP
            grad[c, pl.ds(r * BCD, BCD)] = total.astype(jnp.bfloat16)
            return 0

        lax.fori_loop(0, BR, add, 0)

        def pack(i, _):
            for j in range(SLOTS):
                snd[c, i * SLOTS + j] = grad[c, inv[i * SLOTS + j]]
            return 0

        lax.fori_loop(0, NF, pack, 0)
        for k in range(1, NF):
            dst = (me + k) % NF
            a_cp[c, k] = remote(
                snd.at[c, pl.ds(dst * SLOTS, SLOTS)], rcv.at[c, me],
                a_s.at[c, k], a_r.at[c, k], {"fsdp": dst},
            )
        rcv[c, me] = snd[c, pl.ds(me * SLOTS, SLOTS)]

    send_far(0)
    send_far(1)
    send_raw(0)
    send_com(0)
    send_far(2)
    send_raw(1)
    for cp in loads:
        cp.start()
    send_com(1)
    finish(0)
    send_far(3)
    send_raw(2)
    send_com(2)
    finish(1)
    send_raw(3)
    send_com(3)
    exchange(0)
    finish(2)
    finish(3)
    exchange(1)

    for c in range(2):
        for k in range(1, NF):
            a_cp[c, k].wait_recv()
    for cp in loads:
        cp.wait()

    def block(s):
        halves = [
            rcv[c, :, s].astype(jnp.float32).reshape(B, HALF).astype(jnp.bfloat16) for c in range(2)
        ]
        return jnp.concatenate(halves, axis=1)

    b_cp = {}
    for s in range(SLOTS):
        g = block(s)
        half = jnp.dot(lv[s], g, preferred_element_type=jnp.float32).astype(jnp.bfloat16)
        u = jnp.dot(half, rv[s], preferred_element_type=jnp.float32).astype(jnp.bfloat16)
        ret[:, s] = u.astype(jnp.float32).reshape(NF, ROWS, B).astype(jnp.bfloat16)
        if s % 2 == 1:
            p = s // 2
            for k in range(1, NF):
                dst = (me + k) % NF
                b_cp[p, k] = remote(
                    ret.at[dst, pl.ds(2 * p, 2)], back.at[pl.ds(me * SLOTS + 2 * p, 2)],
                    b_s.at[p, k], b_r.at[p, k], {"fsdp": dst},
                )
            back[pl.ds(me * SLOTS + 2 * p, 2)] = ret[me, pl.ds(2 * p, 2)]

    outs = []
    for s in range(SLOTS):
        g = block(s)
        keep, gain = coef[0, s], coef[1, s]
        left = lax.dot_general(g, g, (((1,), (1,)), ((), ())), preferred_element_type=jnp.float32)
        nlv[s] = keep * lsv[s] + gain * left
        outs.append(pltpu.make_async_copy(nlv.at[s], nl.at[s], out_s.at[0, s]))
        outs[-1].start()
        right = lax.dot_general(g, g, (((0,), (0,)), ((), ())), preferred_element_type=jnp.float32)
        nrv[s] = keep * rsv[s] + gain * right
        outs.append(pltpu.make_async_copy(nrv.at[s], nr.at[s], out_s.at[1, s]))
        outs[-1].start()

    for k in range(4):
        for d in range(2):
            far_cp[k, d].wait_send()
            raw_cp[k, d].wait_send()
            com_cp[k, d].wait_send()
    for c in range(2):
        z_cp[c].wait_send()
        for k in range(1, NF):
            a_cp[c, k].wait_send()
    for p in range(SLOTS // 2):
        for k in range(1, NF):
            b_cp[p, k].wait()
    for cp in outs:
        cp.wait()

    def unpack(i, _):
        for j in range(BCD):
            upd[i, j] = back[own[i * BCD + j]]
        return 0

    lax.fori_loop(0, BR, unpack, 0)


def body(partial_grads, owners, left_roots, right_roots, left_stats, right_stats):
    dp = lax.axis_index("dp")
    me = lax.axis_index("fsdp")
    own = lax.dynamic_slice_in_dim(owners, dp * BCD, BCD, 1).reshape(-1)
    slots = jnp.arange(NF * SLOTS, dtype=jnp.int32)
    hit = slots[:, None] == own[None, :]
    inv = jnp.sum(jnp.where(hit, jnp.arange(NBG, dtype=jnp.int32)[None, :], 0), axis=1, dtype=jnp.int32)
    mine = me * SLOTS + jnp.arange(SLOTS, dtype=jnp.int32)
    occupied = jnp.any(mine[:, None] == own[None, :], axis=1)
    coef = jnp.stack(
        [jnp.where(occupied, DECAY, 1.0), jnp.where(occupied, 1.0 - DECAY, 0.0)]
    ).astype(jnp.float32)
    bf, f32 = jnp.bfloat16, jnp.float32
    any_ = pl.BlockSpec(memory_space=pl.ANY)
    smem = pl.BlockSpec(memory_space=pltpu.SMEM)
    vmem = pl.BlockSpec(memory_space=pltpu.VMEM)
    dma = pltpu.SemaphoreType.DMA
    unit = (4, 2, HR, BCD, ROWS, HALF)
    upd, nl, nr = pl.pallas_call(
        kernel,
        out_shape=(
            jax.ShapeDtypeStruct((BR, BCD, ROWS, B), bf),
            jax.ShapeDtypeStruct((SLOTS, B, B), f32),
            jax.ShapeDtypeStruct((SLOTS, B, B), f32),
        ),
        in_specs=[any_, smem, smem, smem, any_, any_, any_, any_],
        out_specs=(vmem, any_, any_),
        scratch_shapes=[
            pltpu.VMEM(unit, bf), pltpu.VMEM(unit, bf), pltpu.VMEM(unit, bf), pltpu.VMEM(unit, bf),
            pltpu.VMEM(unit, bf),
            pltpu.VMEM((4, BR, BCD, ROWS, HALF), bf),
            pltpu.VMEM((2, BR, BCD, ROWS, HALF), f32),
            pltpu.VMEM((2, BR, BCD, ROWS, HALF), bf),
            pltpu.VMEM((2, BR, BCD, ROWS, HALF), bf),
            pltpu.VMEM((2, NBG, ROWS, HALF), bf),
            pltpu.VMEM((2, NF * SLOTS, ROWS, HALF), bf),
            pltpu.VMEM((2, NF, SLOTS, ROWS, HALF), bf),
            pltpu.VMEM((NF, SLOTS, ROWS, B), bf),
            pltpu.VMEM((NF * SLOTS, ROWS, B), bf),
            pltpu.VMEM((SLOTS, B, B), bf), pltpu.VMEM((SLOTS, B, B), bf),
            pltpu.VMEM((SLOTS, B, B), f32), pltpu.VMEM((SLOTS, B, B), f32),
            pltpu.VMEM((SLOTS, B, B), f32), pltpu.VMEM((SLOTS, B, B), f32),
            dma((4, 2)), dma((4, 2)), dma((4, 2)), dma((4, 2)), dma((4, 2)), dma((4, 2)),
            dma((4, 2)), dma((4,)), dma((2,)), dma((2,)),
            dma((2, NF)), dma((2, NF)), dma((3, NF)), dma((3, NF)), dma((4,)), dma((2, SLOTS)),
        ],
        compiler_params=pltpu.CompilerParams(
            collective_id=0, has_side_effects=True, vmem_limit_bytes=48 * 2**20
        ),
        name="step",
    )(
        partial_grads[0], inv, own, coef,
        left_roots[0], right_roots[0], left_stats[0], right_stats[0],
    )
    return upd, nl[None], nr[None]


def solution(mesh):
    placed = (
        P("dp", None, None, "fsdp", None),
        P(),
        P("dp", "fsdp", None, None),
        P("dp", "fsdp", None, None),
        P("dp", "fsdp", None, None),
        P("dp", "fsdp", None, None),
    )
    return jax.shard_map(
        body,
        mesh=mesh,
        in_specs=placed,
        out_specs=(
            P(None, "dp", "fsdp", None),
            P("dp", "fsdp", None, None),
            P("dp", "fsdp", None, None),
        ),
        check_vma=False,
    )
```

time: 264 us -> 94.6 us (0.36)
  waiting for transfers between devices: 199 us -> 0 us
  Pallas kernels: 0 us -> 87.3 us
  blocking collectives: 34.2 us -> 0 us
  between operations: 14.8 us -> 0.69 us
  matrix products: 6.32 us -> 0 us
  starting transfers between devices: 4.66 us -> 0 us
  local copies, waits for them, and re-layouts: 3.3 us -> 6.15 us
    unnamed x2 -> x0, waiting for transfers between devices: 183 us -> none
    pallas_call x0 -> x1, Pallas kernels: none -> 87.3 us  [body(): pl.pallas_call(kernel, out_shape=(jax.ShapeDtypeStruct((BR, BCD, ROWS, B)...]
    all_to_all x1 -> x0, blocking collectives: 34.2 us -> none  [body(): lax.all_to_all(packed, 'fsdp', split_axis=1, concat_axis=1, tiled=True)]
    all_to_all x1 -> x0, waiting for transfers between devices: 16.5 us -> none  [body(): lax.all_to_all(update, 'fsdp', split_axis=1, concat_axis=1, tiled=True)]
    dot_general x5 -> x0, matrix products: 6.32 us -> none  [the longest x1 3.2 us: body(): jnp.einsum('sji,sjk->sik', blocks, blocks, preferred_element_type=jnp.flo...]
    all_to_all x1 -> x0, starting transfers between devices: 4.62 us -> none  [body(): lax.all_to_all(update, 'fsdp', split_axis=1, concat_axis=1, tiled=True)]
    unnamed x15 -> x9, local copies, waits for them, and re-layouts: 2.01 us -> 5.99 us
  transfers between devices with their start and end apart: 2 -> 0, of which waited for: 2 -> 0; matrix products, arithmetic and copies ran while one was open for 2% -> 0% of each run, Pallas kernels for 0% -> 0%
where the time goes in v1:
time: 94.6 us; the launch traced here: 94.4 us
  Pallas kernels  87.3 us (92%)
  local copies, waits for them, and re-layouts  6.15 us (7%)
    pallas_call x1, Pallas kernels, body(): pl.pallas_call(kernel, out_shape=(jax.ShapeDtypeStruct((BR, BCD, ROWS, B)...  87.3 us
    unnamed x9, local copies, waits for them, and re-layouts  5.99 us

profile of v1, /device:TPU:1, one launch (start us, length us, event | category | flops | bytes accessed | tf_op | source)
XLA Modules:
  0.0 94.4 jit_solution(382283513064536560)
XLA Ops:
  0.6 0.0 copy-start
  0.7 0.7 copy-done
  1.3 0.1 constant_dynamic-slice_fusion
  1.4 0.1 eq.29.own
  1.5 0.2 compare_reduce_fusion
  1.7 0.1 select_reduce_fusion.inv
  1.8 0.0 copy-start.1
  1.8 1.1 %copy-done.1 = bf16[1,6,256,256]{3,2,1,0:T(8,128)(2,1)S(1)} copy-done((bf16[1,6,256,256]{3,2,1,0:T(8,128)(2,1)S(1)}, bf16[1,6,256,256]{3,2,1,0:T(8,128)(2,1)}, u32[]{:S(2)}) %copy-start.1) | copy-done | bytes 786456
  3.0 0.0 copy-start.2
  3.0 1.1 %copy-done.2 = bf16[1,6,256,256]{3,2,1,0:T(8,128)(2,1)S(1)} copy-done((bf16[1,6,256,256]{3,2,1,0:T(8,128)(2,1)S(1)}, bf16[1,6,256,256]{3,2,1,0:T(8,128)(2,1)}, u32[]{:S(2)}) %copy-start.2) | copy-done | bytes 786456
  4.1 87.3 %step.1 = (bf16[16,7,8,256]{3,2,1,0:T(8,128)(2,1)S(1)}, f32[6,256,256]{2,1,0:T(8,128)S(1)}, f32[6,256,256]{2,1,0:T(8,128)S(1)}) custom-call(bf16[16,56,8,256]{3,2,1,0:T(8,128)(2,1)} %bitcast.15, s32[192]{0:T(256)S(1)} %select_reduce_fusion.inv, s32[112]{0:T(128)S(1)} %eq.29.own, f32[2,6]{1,0:T(2,128)S(1)} %pad_maximum_fusion.coef, ...), custom_call_target="tpu_custom_call" | custom-call | tf_op jit(solution)/shard_map/step/pallas_call | solution.py:251
  91.4 0.8 copy.12
  92.1 1.1 %copy.13 = f32[1,6,256,256]{3,2,1,0:T(8,128)} copy(f32[1,6,256,256]{3,2,1,0:T(8,128)S(1)} %bitcast.12) | data formatting | bytes 3145728
  93.3 1.1 %copy.14 = f32[1,6,256,256]{3,2,1,0:T(8,128)} copy(f32[1,6,256,256]{3,2,1,0:T(8,128)S(1)} %bitcast.11) | data formatting | bytes 3145728
  (3 shorter events, 0.0 us)
Async XLA Ops:
  0.6 0.7 copy-start
  1.8 1.1 %copy-start.1 = (bf16[1,6,256,256]{3,2,1,0:T(8,128)(2,1)S(1)}, bf16[1,6,256,256]{3,2,1,0:T(8,128)(2,1)}, u32[]{:S(2)}) copy-start(bf16[1,6,256,256]{3,2,1,0:T(8,128)(2,1)} %param.8) | copy-start | bytes 2359300
  3.0 1.1 %copy-start.2 = (bf16[1,6,256,256]{3,2,1,0:T(8,128)(2,1)S(1)}, bf16[1,6,256,256]{3,2,1,0:T(8,128)(2,1)}, u32[]{:S(2)}) copy-start(bf16[1,6,256,256]{3,2,1,0:T(8,128)(2,1)} %param.9) | copy-start | bytes 2359300

commit v2 on v1

v2 whole, which is shorter than its diff:
```python
import jax
import jax.numpy as jnp
from jax import lax
from jax.experimental import pallas as pl
from jax.experimental.pallas import tpu as pltpu
from jax.sharding import PartitionSpec as P

MESH = pl.DeviceIdType.MESH
DECAY = 0.95
BR, BCD, ROWS, B = 16, 7, 8, 256
NBG, SLOTS, NF, NY, NDP = 112, 6, 32, 4, 8
HALF = B // 2
HR = BR // 2
Q = 2
HQ = HR // Q
LEAD = 2


def kernel(
    pg, owners, lroot, rroot, lstat, rstat,
    upd, nl, nr,
    far, raw, com, mix, near, mine, part, zout, zin_a, zin_b, snd, rcv, ret, back, table, inv, own,
    lv, rv, lsv, rsv, nlv, nrv,
    far_s, far_r, raw_s, raw_r, com_s, com_r, near_s, mine_s, z_s, z_r,
    a_s, a_r, b_s, b_r, load_s, out_s, table_s, own_s,
):
    zin = (zin_a, zin_b)
    dp = lax.axis_index("dp")
    me = lax.axis_index("fsdp")
    zh, y = dp // NY, dp % NY
    up, down = (y + 1) % NY, (y + 3) % NY
    over = (y + 2) % NY
    to = (zh * NY + up, zh * NY + down)
    across = (1 - zh) * NY + y

    barrier = pltpu.get_barrier_semaphore()
    for d in to + (across,):
        pl.semaphore_signal(barrier, inc=1, device_id={"dp": d}, device_id_type=MESH)
    for k in range(1, NF):
        pl.semaphore_signal(
            barrier, inc=1, device_id={"fsdp": (me + k) % NF}, device_id_type=MESH
        )

    def cut(c, h, rows, target):
        side = 1 - zh if h == 0 else zh
        g = side * NY + target
        return pg.at[rows, pl.ds(g * BCD, BCD), :, pl.ds(c * HALF, HALF)]

    own_cp = pltpu.make_async_copy(owners, own, own_s)
    own_cp.start()

    units = [(c, h, q) for h in range(2) for c in range(2) for q in range(Q)]
    n_units = len(units)

    def rows(q, d):
        return pl.ds(d * HR + q * HQ, HQ)

    near_cp, mine_cp = {}, {}
    for u, (c, h, q) in enumerate(units):
        for d, target in enumerate((up, down)):
            near_cp[u, d] = pltpu.make_async_copy(
                cut(c, h, rows(q, d), target), near.at[u, d], near_s.at[u, d]
            )
            near_cp[u, d].start()
            mine_cp[u, d] = pltpu.make_async_copy(
                cut(c, h, rows(q, d), y), mine.at[u, d], mine_s.at[u, d]
            )
            mine_cp[u, d].start()
    loads = [
        pltpu.make_async_copy(src, dst, load_s.at[i])
        for i, (src, dst) in enumerate(((lroot, lv), (rroot, rv), (lstat, lsv), (rstat, rsv)))
    ]

    pl.semaphore_wait(barrier, 3 + NF - 1)

    def remote(src, dst, s, r, device):
        cp = pltpu.make_async_remote_copy(
            src_ref=src, dst_ref=dst, send_sem=s, recv_sem=r, device_id=device, device_id_type=MESH
        )
        cp.start()
        return cp

    far_cp, raw_cp, com_cp, z_cp = {}, {}, {}, {}

    def send_far(u):
        if u >= n_units:
            return
        c, h, q = units[u]
        for d in range(2):
            far_cp[u, d] = remote(
                cut(c, h, rows(q, d), over), far.at[u, d], far_s.at[u, d], far_r.at[u, d],
                {"dp": to[d]},
            )

    def send_raw(u):
        if u >= n_units:
            return
        c, h, q = units[u]
        for d, target in enumerate((up, down)):
            raw_cp[u, d] = remote(
                cut(c, h, rows(q, 1 - d), target), raw.at[u, d], raw_s.at[u, d], raw_r.at[u, d],
                {"dp": to[d]},
            )

    def send_com(u):
        for d in range(2):
            near_cp[u, d].wait()
            far_cp[u, d].wait_recv()

            def add(i, _):
                mix[u, d, i] = far[u, d, i] + near[u, d, i]
                return 0

            lax.fori_loop(0, HQ, add, 0)
            com_cp[u, d] = remote(
                mix.at[u, d], com.at[u, d], com_s.at[u, d], com_r.at[u, d], {"dp": to[d]}
            )

    def finish(u):
        c, h, q = units[u]
        for d in range(2):
            mine_cp[u, d].wait()
            raw_cp[u, d].wait_recv()
            com_cp[u, d].wait_recv()
        f32 = jnp.float32

        def add(i, _):
            for d in range(2):
                total = mine[u, d, i].astype(f32) + com[u, d, i].astype(f32)
                total = total + raw[u, 1 - d, i].astype(f32)
                at = pl.ds(((q * 2 + d) * HQ + i) * BCD, BCD)
                if h == 0:
                    zout[c, at] = total.astype(jnp.bfloat16)
                else:
                    part[c, at] = total
            return 0

        lax.fori_loop(0, HQ, add, 0)
        if h == 0:
            at = pl.ds(q * (NBG // Q), NBG // Q)
            z_cp[c, q] = remote(
                zout.at[c, at], zin[c].at[at], z_s.at[c, q], z_r.at[c, q], {"dp": across}
            )

    def owner_copy(c, k):
        dst = (me + k) % NF
        return pltpu.make_async_remote_copy(
            src_ref=snd.at[c, pl.ds(dst * SLOTS, SLOTS)], dst_ref=rcv.at[c, me],
            send_sem=a_s.at[c, k], recv_sem=a_r.at[c, k],
            device_id={"fsdp": dst}, device_id_type=MESH,
        )

    def return_copy(p, k):
        dst = (me + k) % NF
        return pltpu.make_async_remote_copy(
            src_ref=ret.at[dst, pl.ds(2 * p, 2)], dst_ref=back.at[pl.ds(me * SLOTS + 2 * p, 2)],
            send_sem=b_s.at[p, k], recv_sem=b_r.at[p, k],
            device_id={"fsdp": dst}, device_id_type=MESH,
        )

    def each(act):
        def go(k, _):
            act(k)
            return 0

        lax.fori_loop(1, NF, go, 0)

    def pack(c, dst):
        for j in range(SLOTS):
            e = jnp.maximum(inv[dst, j], 0)
            total = (part[c, e] + zin[c][e].astype(jnp.float32)) * (1.0 / NDP)
            snd[c, dst * SLOTS + j] = total.astype(jnp.bfloat16)

    def exchange(c):
        for q in range(Q):
            z_cp[c, q].wait_recv()

        def go(k):
            pack(c, (me + k) % NF)
            owner_copy(c, k).start()

        each(go)
        pack(c, me)
        rcv[c, me] = snd[c, pl.ds(me * SLOTS, SLOTS)]

    for u in range(LEAD):
        send_far(u)
    send_raw(0)

    own_cp.wait()
    lane = lax.broadcasted_iota(jnp.int32, (NF, 128), 1)
    slot = lax.broadcasted_iota(jnp.int32, (NF, 128), 0) * SLOTS + lane
    slot = jnp.where(lane < SLOTS, slot, -1)

    def enter(r, held):
        d, q, i = r // HR, r % HR // HQ, r % HQ
        first = ((q * 2 + d) * HQ + i) * BCD
        for b in range(BCD):
            held = jnp.where(slot == own[r, dp * BCD + b], first + b, held)
        return held

    table[...] = lax.fori_loop(0, BR, enter, jnp.full((NF, 128), -1, jnp.int32))
    table_cp = pltpu.make_async_copy(table, inv, table_s)
    table_cp.start()

    for u in range(n_units):
        send_com(u)
        send_far(u + LEAD)
        send_raw(u + 1)
        if u == LEAD:
            for cp in loads:
                cp.start()
        if u >= 1:
            finish(u - 1)
        if u - 1 == 3 * Q - 1:
            table_cp.wait()
            exchange(0)
    finish(n_units - 1)
    exchange(1)

    for c in range(2):
        each(lambda k: owner_copy(c, k).wait_recv())
    for cp in loads:
        cp.wait()

    def block(s):
        halves = [
            rcv[c, :, s].astype(jnp.float32).reshape(B, HALF).astype(jnp.bfloat16) for c in range(2)
        ]
        return jnp.concatenate(halves, axis=1)

    def work(p, _):
        for j in range(2):
            s = 2 * p + j
            g = block(s)
            half = jnp.dot(lv[s], g, preferred_element_type=jnp.float32).astype(jnp.bfloat16)
            u = jnp.dot(half, rv[s], preferred_element_type=jnp.float32).astype(jnp.bfloat16)
            ret[:, s] = u.astype(jnp.float32).reshape(NF, ROWS, B).astype(jnp.bfloat16)
        each(lambda k: return_copy(p, k).start())
        back[pl.ds(me * SLOTS + 2 * p, 2)] = ret[me, pl.ds(2 * p, 2)]
        return 0

    lax.fori_loop(0, SLOTS // 2, work, 0)

    def out_copies(s):
        return [
            pltpu.make_async_copy(nlv.at[s], nl.at[s], out_s.at[0, s]),
            pltpu.make_async_copy(nrv.at[s], nr.at[s], out_s.at[1, s]),
        ]

    def statistics(s, _):
        g = block(s)
        held = inv[me, s] >= 0
        keep = jnp.where(held, jnp.float32(DECAY), jnp.float32(1.0))
        gain = jnp.where(held, jnp.float32(1.0 - DECAY), jnp.float32(0.0))
        left = lax.dot_general(g, g, (((1,), (1,)), ((), ())), preferred_element_type=jnp.float32)
        nlv[s] = keep * lsv[s] + gain * left
        right = lax.dot_general(g, g, (((0,), (0,)), ((), ())), preferred_element_type=jnp.float32)
        nrv[s] = keep * rsv[s] + gain * right
        for cp in out_copies(s):
            cp.start()
        return 0

    lax.fori_loop(0, SLOTS, statistics, 0)

    for u in range(n_units):
        for d in range(2):
            far_cp[u, d].wait_send()
            raw_cp[u, d].wait_send()
            com_cp[u, d].wait_send()
    for c in range(2):
        for q in range(Q):
            z_cp[c, q].wait_send()
        each(lambda k: owner_copy(c, k).wait_send())
    for s in range(SLOTS):
        for cp in out_copies(s):
            cp.wait()
    for p in range(SLOTS // 2):
        each(lambda k: return_copy(p, k).wait())

    def unpack(i, _):
        for j in range(BCD):
            upd[i, j] = back[own[i, dp * BCD + j]]
        return 0

    lax.fori_loop(0, BR, unpack, 0)


def body(partial_grads, owners, left_roots, right_roots, left_stats, right_stats):
    bf, f32 = jnp.bfloat16, jnp.float32
    any_ = pl.BlockSpec(memory_space=pl.ANY)
    hbm = pl.BlockSpec(memory_space=pltpu.HBM)
    vmem = pl.BlockSpec(memory_space=pltpu.VMEM)
    dma = pltpu.SemaphoreType.DMA
    unit = (4 * Q, 2, HQ, BCD, ROWS, HALF)
    piece = (2, NBG, ROWS, HALF)
    pair = (4 * Q, 2)
    upd, nl, nr = pl.pallas_call(
        kernel,
        out_shape=(
            jax.ShapeDtypeStruct((BR, BCD, ROWS, B), bf),
            jax.ShapeDtypeStruct((SLOTS, B, B), f32),
            jax.ShapeDtypeStruct((SLOTS, B, B), f32),
        ),
        in_specs=[hbm, hbm, hbm, hbm, hbm, hbm],
        out_specs=(vmem, any_, any_),
        scratch_shapes=[
            pltpu.VMEM(unit, bf), pltpu.VMEM(unit, bf), pltpu.VMEM(unit, bf), pltpu.VMEM(unit, bf),
            pltpu.VMEM(unit, bf),
            pltpu.VMEM(unit, bf),
            pltpu.VMEM(piece, f32), pltpu.VMEM(piece, bf),
            pltpu.VMEM(piece[1:], bf), pltpu.VMEM(piece[1:], bf),
            pltpu.VMEM((2, NF * SLOTS, ROWS, HALF), bf),
            pltpu.VMEM((2, NF, SLOTS, ROWS, HALF), bf),
            pltpu.VMEM((NF, SLOTS, ROWS, B), bf),
            pltpu.VMEM((NF * SLOTS, ROWS, B), bf),
            pltpu.VMEM((NF, 128), jnp.int32), pltpu.SMEM((NF, 128), jnp.int32),
            pltpu.SMEM((BR, BCD * NDP), jnp.int32),
            pltpu.VMEM((SLOTS, B, B), bf), pltpu.VMEM((SLOTS, B, B), bf),
            pltpu.VMEM((SLOTS, B, B), f32), pltpu.VMEM((SLOTS, B, B), f32),
            pltpu.VMEM((SLOTS, B, B), f32), pltpu.VMEM((SLOTS, B, B), f32),
            dma(pair), dma(pair), dma(pair), dma(pair), dma(pair), dma(pair),
            dma(pair), dma(pair), dma((2, Q)), dma((2, Q)),
            dma((2, NF)), dma((2, NF)), dma((3, NF)), dma((3, NF)), dma((4,)), dma((2, SLOTS)), dma, dma,
        ],
        compiler_params=pltpu.CompilerParams(
            collective_id=0, has_side_effects=True, vmem_limit_bytes=48 * 2**20
        ),
        name="step",
    )(
        partial_grads[0],
        *(
            pltpu.with_memory_space_constraint(x[0], pltpu.HBM)
            for x in (owners[None], left_roots, right_roots, left_stats, right_stats)
        ),
    )
    return upd, nl[None], nr[None]


def solution(mesh):
    placed = (
        P("dp", None, None, "fsdp", None),
        P(),
        P("dp", "fsdp", None, None),
        P("dp", "fsdp", None, None),
        P("dp", "fsdp", None, None),
        P("dp", "fsdp", None, None),
    )
    return jax.shard_map(
        body,
        mesh=mesh,
        in_specs=placed,
        out_specs=(
            P(None, "dp", "fsdp", None),
            P("dp", "fsdp", None, None),
            P("dp", "fsdp", None, None),
        ),
        check_vma=False,
    )
```

time: 94.6 us -> 84 us (0.89)
  Pallas kernels: 87.3 us -> 80.2 us
  local copies, waits for them, and re-layouts: 6.15 us -> 3.05 us
    pallas_call x1, Pallas kernels: 87.3 us -> 80.2 us  [body(): pl.pallas_call(kernel, out_shape=(jax.ShapeDtypeStruct((BR, BCD, ROWS, B)...]
    unnamed x9 -> x3, local copies, waits for them, and re-layouts: 5.99 us -> 3.05 us
where the time goes in v2:
time: 84 us; the launch traced here: 83.9 us
  Pallas kernels  80.2 us (95%)
  local copies, waits for them, and re-layouts  3.05 us (4%)
    pallas_call x1, Pallas kernels, body(): pl.pallas_call(kernel, out_shape=(jax.ShapeDtypeStruct((BR, BCD, ROWS, B)...  80.2 us
    unnamed x3, local copies, waits for them, and re-layouts  3.05 us

profile of v2, /device:TPU:1, one launch (start us, length us, event | category | flops | bytes accessed | tf_op | source)
XLA Modules:
  0.0 83.9 jit_solution(933495789373598617)
XLA Ops:
  0.6 80.2 %step.1 = (bf16[16,7,8,256]{3,2,1,0:T(8,128)(2,1)S(1)}, f32[6,256,256]{2,1,0:T(8,128)S(1)}, f32[6,256,256]{2,1,0:T(8,128)S(1)}) custom-call(bf16[16,56,8,256]{3,2,1,0:T(8,128)(2,1)} %bitcast.9, s32[16,56]{1,0:T(8,128)} %owners.1, bf16[6,256,256]{2,1,0:T(8,128)(2,1)} %bitcast.12, bf16[6,256,256]{2,1,0:T(8,128)(2,1)} %bitcast.13, f32[6,256,256]{2,1,0:T(8,128)} %bitcast.10, ...), custom_call_target="tpu_custom_call" | custom-call | tf_op jit(solution)/shard_map/step/pallas_call | solution.py:298
  80.9 0.8 copy.12
  81.6 1.1 %copy.13 = f32[1,6,256,256]{3,2,1,0:T(8,128)} copy(f32[1,6,256,256]{3,2,1,0:T(8,128)S(1)} %bitcast.8) | data formatting | bytes 3145728
  82.8 1.1 %copy.14 = f32[1,6,256,256]{3,2,1,0:T(8,128)} copy(f32[1,6,256,256]{3,2,1,0:T(8,128)S(1)} %bitcast.7) | data formatting | bytes 3145728

commit v3 on v2

--- a/solution.py
+++ b/solution.py
@@ -22,7 +22,7 @@
     far, raw, com, mix, near, mine, part, zout, zin_a, zin_b, snd, rcv, ret, back, table, inv, own,
     lv, rv, lsv, rsv, nlv, nrv,
     far_s, far_r, raw_s, raw_r, com_s, com_r, near_s, mine_s, z_s, z_r,
-    a_s, a_r, b_s, b_r, load_s, out_s, table_s, own_s,
+    a_s, a_r, b_s, b_r, load_s, out_s, table_s, own_s, ready,
 ):
     zin = (zin_a, zin_b)
     dp = lax.axis_index("dp")
@@ -36,10 +36,10 @@
     barrier = pltpu.get_barrier_semaphore()
     for d in to + (across,):
         pl.semaphore_signal(barrier, inc=1, device_id={"dp": d}, device_id_type=MESH)
-    for k in range(1, NF):
-        pl.semaphore_signal(
-            barrier, inc=1, device_id={"fsdp": (me + k) % NF}, device_id_type=MESH
-        )
+    bits = [1 << b for b in range(NF.bit_length() - 1)]
+    mates = [me + bit * (1 - 2 * (me // bit % 2)) for bit in bits]
+    for mate in mates:
+        pl.semaphore_signal(barrier, inc=1, device_id={"fsdp": mate}, device_id_type=MESH)
 
     def cut(c, h, rows, target):
         side = 1 - zh if h == 0 else zh
@@ -71,7 +71,7 @@
         for i, (src, dst) in enumerate(((lroot, lv), (rroot, rv), (lstat, lsv), (rstat, rsv)))
     ]
 
-    pl.semaphore_wait(barrier, 3 + NF - 1)
+    pl.semaphore_wait(barrier, 3 + len(mates))
 
     def remote(src, dst, s, r, device):
         cp = pltpu.make_async_remote_copy(
@@ -153,7 +153,7 @@
     def return_copy(p, k):
         dst = (me + k) % NF
         return pltpu.make_async_remote_copy(
-            src_ref=ret.at[dst, pl.ds(2 * p, 2)], dst_ref=back.at[pl.ds(me * SLOTS + 2 * p, 2)],
+            src_ref=ret.at[dst, pl.ds(6 * p, 6)], dst_ref=back.at[pl.ds(me * SLOTS + 6 * p, 6)],
             send_sem=b_s.at[p, k], recv_sem=b_r.at[p, k],
             device_id={"fsdp": dst}, device_id_type=MESH,
         )
@@ -203,7 +203,15 @@
     table_cp = pltpu.make_async_copy(table, inv, table_s)
     table_cp.start()
 
+    def greet(b):
+        pl.semaphore_signal(ready.at[b], inc=1, device_id={"fsdp": mates[b]}, device_id_type=MESH)
+
+    greet(1)
     for u in range(n_units):
+        if 0 < u < len(mates):
+            pl.semaphore_wait(ready.at[u], 1)
+            if u + 1 < len(mates):
+                greet(u + 1)
         send_com(u)
         send_far(u + LEAD)
         send_raw(u + 1)
@@ -230,17 +238,17 @@
         return jnp.concatenate(halves, axis=1)
 
     def work(p, _):
-        for j in range(2):
-            s = 2 * p + j
+        for j in range(6):
+            s = 6 * p + j
             g = block(s)
             half = jnp.dot(lv[s], g, preferred_element_type=jnp.float32).astype(jnp.bfloat16)
             u = jnp.dot(half, rv[s], preferred_element_type=jnp.float32).astype(jnp.bfloat16)
             ret[:, s] = u.astype(jnp.float32).reshape(NF, ROWS, B).astype(jnp.bfloat16)
         each(lambda k: return_copy(p, k).start())
-        back[pl.ds(me * SLOTS + 2 * p, 2)] = ret[me, pl.ds(2 * p, 2)]
+        back[pl.ds(me * SLOTS + 6 * p, 6)] = ret[me, pl.ds(6 * p, 6)]
         return 0
 
-    lax.fori_loop(0, SLOTS // 2, work, 0)
+    lax.fori_loop(0, SLOTS // 6, work, 0)
 
     def out_copies(s):
         return [
@@ -275,7 +283,7 @@
     for s in range(SLOTS):
         for cp in out_copies(s):
             cp.wait()
-    for p in range(SLOTS // 2):
+    for p in range(SLOTS // 6):
         each(lambda k: return_copy(p, k).wait())
 
     def unpack(i, _):
@@ -322,6 +330,7 @@
             dma(pair), dma(pair), dma(pair), dma(pair), dma(pair), dma(pair),
             dma(pair), dma(pair), dma((2, Q)), dma((2, Q)),
             dma((2, NF)), dma((2, NF)), dma((3, NF)), dma((3, NF)), dma((4,)), dma((2, SLOTS)), dma, dma,
+            pltpu.SemaphoreType.REGULAR((5,)),
         ],
         compiler_params=pltpu.CompilerParams(
             collective_id=0, has_side_effects=True, vmem_limit_bytes=48 * 2**20

time: 84 us -> 81.8 us (0.974)
  the two profiles are of different devices: /device:TPU:1 before, /device:TPU:39 now
where the time goes in v3:
time: 81.8 us; the launch traced here: 81.7 us
  Pallas kernels  78 us (95%)
  local copies, waits for them, and re-layouts  3.05 us (4%)
    pallas_call x1, Pallas kernels, body(): pl.pallas_call(kernel, out_shape=(jax.ShapeDtypeStruct((BR, BCD, ROWS, B)...  78 us
    unnamed x3, local copies, waits for them, and re-layouts  3.05 us

profile of v3, /device:TPU:39, one launch (start us, length us, event | category | flops | bytes accessed | tf_op | source)
XLA Modules:
  0.0 81.7 jit_solution(5626412776119818244)
XLA Ops:
  0.6 78.0 %step.1 = (bf16[16,7,8,256]{3,2,1,0:T(8,128)(2,1)S(1)}, f32[6,256,256]{2,1,0:T(8,128)S(1)}, f32[6,256,256]{2,1,0:T(8,128)S(1)}) custom-call(bf16[16,56,8,256]{3,2,1,0:T(8,128)(2,1)} %bitcast.9, s32[16,56]{1,0:T(8,128)} %owners.1, bf16[6,256,256]{2,1,0:T(8,128)(2,1)} %bitcast.12, bf16[6,256,256]{2,1,0:T(8,128)(2,1)} %bitcast.13, f32[6,256,256]{2,1,0:T(8,128)} %bitcast.10, ...), custom_call_target="tpu_custom_call" | custom-call | tf_op jit(solution)/shard_map/step/pallas_call | solution.py:306
  78.7 0.8 copy.12
  79.4 1.1 %copy.13 = f32[1,6,256,256]{3,2,1,0:T(8,128)} copy(f32[1,6,256,256]{3,2,1,0:T(8,128)S(1)} %bitcast.8) | data formatting | bytes 3145728
  80.6 1.1 %copy.14 = f32[1,6,256,256]{3,2,1,0:T(8,128)} copy(f32[1,6,256,256]{3,2,1,0:T(8,128)S(1)} %bitcast.7) | data formatting | bytes 3145728

commit v4 on v3

--- a/solution.py
+++ b/solution.py
@@ -213,8 +213,8 @@
             if u + 1 < len(mates):
                 greet(u + 1)
         send_com(u)
+        send_raw(u + 1)
         send_far(u + LEAD)
-        send_raw(u + 1)
         if u == LEAD:
             for cp in loads:
                 cp.start()

time: 81.8 us -> 81.8 us (level)
  no operation moved by 1% of the time
where the time goes in v4:
time: 81.8 us; the launch traced here: 81.7 us
  Pallas kernels  78 us (95%)
  local copies, waits for them, and re-layouts  3.05 us (4%)
    pallas_call x1, Pallas kernels, body(): pl.pallas_call(kernel, out_shape=(jax.ShapeDtypeStruct((BR, BCD, ROWS, B)...  78 us
    unnamed x3, local copies, waits for them, and re-layouts  3.05 us

profile of v4, /device:TPU:39, one launch (start us, length us, event | category | flops | bytes accessed | tf_op | source)
XLA Modules:
  0.0 81.7 jit_solution(12871518542346596933)
XLA Ops:
  0.6 78.0 %step.1 = (bf16[16,7,8,256]{3,2,1,0:T(8,128)(2,1)S(1)}, f32[6,256,256]{2,1,0:T(8,128)S(1)}, f32[6,256,256]{2,1,0:T(8,128)S(1)}) custom-call(bf16[16,56,8,256]{3,2,1,0:T(8,128)(2,1)} %bitcast.9, s32[16,56]{1,0:T(8,128)} %owners.1, bf16[6,256,256]{2,1,0:T(8,128)(2,1)} %bitcast.12, bf16[6,256,256]{2,1,0:T(8,128)(2,1)} %bitcast.13, f32[6,256,256]{2,1,0:T(8,128)} %bitcast.10, ...), custom_call_target="tpu_custom_call" | custom-call | tf_op jit(solution)/shard_map/step/pallas_call | solution.py:306
  78.7 0.8 copy.12
  79.4 1.1 %copy.13 = f32[1,6,256,256]{3,2,1,0:T(8,128)} copy(f32[1,6,256,256]{3,2,1,0:T(8,128)S(1)} %bitcast.8) | data formatting | bytes 3145728
  80.6 1.1 %copy.14 = f32[1,6,256,256]{3,2,1,0:T(8,128)} copy(f32[1,6,256,256]{3,2,1,0:T(8,128)S(1)} %bitcast.7) | data formatting | bytes 3145728
